TPU v7x, 32 devices: a whole 2x2x4 slice. The times are simulated.
32 devices in a mesh: prow: 8 (over y, x, core), pcol: 4 (over z).
Axes of the slice: x: 2, y: 2, z: 4, core: 2. Of those that a mesh axis runs over, the one named last changes fastest.
Arguments:
- right_sides: float32 [24, 3, 4, 64, 512], P(None, None, None, 'prow', 'pcol'), may hold values from -6 to 6
- modulus: float32 [4, 64, 512], P(None, 'prow', 'pcol'), may hold values from 0.2 to 5
- margin_sides: int32 [8, 4, 4], P('prow', 'pcol'), may hold values 0 or 1
- coarse_vectors: float32 [64, 3, 4, 64, 512], P(None, None, None, 'prow', 'pcol'), may hold values from -0.01953125 to 0.01953125
- coarse_inverse: float32 [4, 64, 64], P('pcol'), may hold values from -3.009933 to 28.092708
Outputs:
- preconditioned: float32 [24, 3, 4, 64, 512], P(None, None, None, 'prow', 'pcol')
All inputs are finite; a program needn't handle non-finite values. No bound on the sum of `margin_sides` on one device may be relied on, other than what follows from the above.
Results may differ from a plain program's by a relative error of at most 0.00005.
Values sent between devices are 32-bit elements; how exact they have to be, the bound alone decides.
A program may use at most 128 MiB of HBM per device.

v0:
```python
import jax
import jax.numpy as jnp
from jax import lax
from jax.sharding import PartitionSpec as P

RELAX_WEIGHT = 0.7
MASS_SHIFT = 0.5
DIAGONAL_SLOPE = 0.6 + 0.4 / 3.0
BOND_TOTAL = 44.0 / 3.0


def extended(x, sides, width):
    for axis, dim in sides:
        size, length = (lax.axis_size(axis), x.shape[dim])
        up = [(i, (i + 1) % size) for i in range(size - 1)]
        down = [(j, i) for i, j in up]
        last = lax.slice_in_dim(x, length - width, length, axis=dim)
        first = lax.slice_in_dim(x, 0, width, axis=dim)
        before = lax.ppermute(last, axis, up)
        after = lax.ppermute(first, axis, down)
        x = jnp.concatenate([before, x, after], axis=dim)
    return x


def bond_sum(field_padded, modulus_padded, factor_rows, factor_columns):
    plane_count = modulus_padded.shape[0] - 2
    row_count = modulus_padded.shape[1] - 2
    column_count = modulus_padded.shape[2] - 2
    own_field = field_padded[..., 1:-1, 1:-1, 1:-1]
    own_modulus = modulus_padded[1:-1, 1:-1, 1:-1]
    accumulated = MASS_SHIFT * own_field
    for step_p in (-1, 0, 1):
        for step_x in (-1, 0, 1):
            for step_y in (-1, 0, 1):
                if step_p == 0 and step_x == 0 and (step_y == 0):
                    continue
                length = step_p * step_p + step_x * step_x + step_y * step_y
                weight = 1.0 / (length * BOND_TOTAL)
                near_field = field_padded[
                    ...,
                    1 + step_p : 1 + step_p + plane_count,
                    1 + step_x : 1 + step_x + row_count,
                    1 + step_y : 1 + step_y + column_count,
                ]
                near_modulus = modulus_padded[
                    1 + step_p : 1 + step_p + plane_count,
                    1 + step_x : 1 + step_x + row_count,
                    1 + step_y : 1 + step_y + column_count,
                ]
                factor = factor_rows[step_x + 1] * factor_columns[step_y + 1]
                difference = own_field - factor * near_field
                bond_weight = 0.5 * weight * (own_modulus + near_modulus)
                direction = (step_p, step_x, step_y)
                projected = 0.0
                for component in range(3):
                    if direction[component] != 0:
                        projected = (
                            projected + direction[component] * difference[..., component, :, :, :]
                        )
                pieces = []
                for component in range(3):
                    piece = 0.6 * difference[..., component, :, :, :]
                    if direction[component] != 0:
                        piece = piece + 0.4 * direction[component] / length * projected
                    pieces.append(piece)
                accumulated = accumulated + bond_weight * jnp.stack(pieces, axis=-4)
    return accumulated


def per_device(right_sides, modulus, margin_sides, coarse_vectors, coarse_inverse):
    load_count = right_sides.shape[0]
    plane_count = right_sides.shape[2]
    row_count = right_sides.shape[3]
    column_count = right_sides.shape[4]
    stacked = jnp.concatenate(
        [right_sides.reshape(load_count * 3, plane_count, row_count, column_count), modulus[None]],
        axis=0,
    )
    padded_all = extended(stacked, (("prow", 2), ("pcol", 3)), 1)
    load_halo = padded_all[: load_count * 3].reshape(
        load_count, 3, plane_count, row_count + 2, column_count + 2
    )
    modulus_halo = padded_all[load_count * 3]
    first_halo = RELAX_WEIGHT * load_halo / (MASS_SHIFT + DIAGONAL_SLOPE * modulus_halo)
    first_padded = jnp.pad(first_halo, ((0, 0), (0, 0), (1, 1), (0, 0), (0, 0)))
    modulus_padded = jnp.pad(modulus_halo, ((1, 1), (0, 0), (0, 0)))
    side_values = margin_sides[0, 0].astype(jnp.float32)
    row_index = lax.broadcasted_iota(jnp.int32, (row_count, column_count), 0)
    column_index = lax.broadcasted_iota(jnp.int32, (row_count, column_count), 1)
    unity = jnp.ones((row_count, column_count), jnp.float32)
    factor_rows = jnp.stack(
        [
            jnp.where(row_index == 0, side_values[0], unity),
            unity,
            jnp.where(row_index == row_count - 1, side_values[1], unity),
        ]
    )
    factor_columns = jnp.stack(
        [
            jnp.where(column_index == 0, side_values[2], unity),
            unity,
            jnp.where(column_index == column_count - 1, side_values[3], unity),
        ]
    )
    diagonal = MASS_SHIFT + DIAGONAL_SLOPE * modulus
    first = first_halo[..., 1:-1, 1:-1]
    applied = bond_sum(first_padded, modulus_padded, factor_rows, factor_columns)
    smoothed = first + RELAX_WEIGHT * (right_sides - applied) / diagonal
    flat_vectors = coarse_vectors.reshape(coarse_vectors.shape[0], -1)
    flat_loads = right_sides.reshape(load_count, -1)
    partial_terms = lax.dot_general(
        flat_vectors, flat_loads, (((1,), (1,)), ((), ())), precision=lax.Precision.HIGHEST
    )
    restricted = lax.psum(partial_terms, "prow")
    solved = jnp.dot(coarse_inverse[0], restricted, precision=lax.Precision.HIGHEST)
    lifted = lax.dot_general(
        solved, flat_vectors, (((0,), (0,)), ((), ())), precision=lax.Precision.HIGHEST
    )
    return smoothed + lifted.reshape(right_sides.shape)


def solution(mesh):
    in_specs = (
        P(None, None, None, "prow", "pcol"),
        P(None, "prow", "pcol"),
        P("prow", "pcol", None),
        P(None, None, None, "prow", "pcol"),
        P("pcol", None, None),
    )
    out_specs = P(None, None, None, "prow", "pcol")
    return jax.shard_map(
        per_device, mesh=mesh, in_specs=in_specs, out_specs=out_specs, check_vma=False
    )
```

profile of v0, /device:TPU:12, one launch (start us, length us, event | category | flops | bytes accessed | tf_op | source)
XLA Modules:
  0.0 149.9 jit_solution(6962504914575081396)
XLA Ops:
  0.0 2.0 %pad_maximum_fusion.3 = (f32[73,4,1,128]{3,2,1,0:T(1,128)S(1)}, f32[73,4,1,128]{3,2,1,0:T(1,128)S(1)}) fusion(f32[1,4,8,128]{3,2,1,0:T(8,128)} %bitcast.43, f32[72,4,8,128]{3,2,1,0:T(8,128)} %bitcast.36), kind=kLoop, calls=%fused_computation.248 | loop fusion | flops 74752 | bytes 1495040 | tf_op jit(solution)/shard_map/slice | solution.py:17
  2.1 2.8 %collective-permute-start.1 = (f32[73,4,1,128]{3,2,1,0:T(1,128)S(1)}, f32[73,4,1,128]{3,2,1,0:T(1,128)S(1)}, u32[]{:S(2)}, u32[]{:S(2)}) collective-permute-start(f32[73,4,1,128]{3,2,1,0:T(1,128)S(1)} %get-tuple-element.80), channel_id=1, source_target_pairs={{4,0},{8,4},{12,8},{16,12},{20,16},{24,20},{28,24},{5,1},{9,5},{13... | collective-permute-start | bytes 448520 | tf_op jit(solution)/shard_map/ppermute | solution.py:20
  4.8 1.9 %collective-permute-start = (f32[73,4,1,128]{3,2,1,0:T(1,128)S(1)}, f32[73,4,1,128]{3,2,1,0:T(1,128)S(1)}, u32[]{:S(2)}, u32[]{:S(2)}) collective-permute-start(f32[73,4,1,128]{3,2,1,0:T(1,128)S(1)} %get-tuple-element.79), channel_id=1, source_target_pairs={{0,4},{4,8},{8,12},{12,16},{16,20},{20,24},{24,28},{1,5},{5,9},{9,... | collective-permute-start | bytes 448520 | tf_op jit(solution)/shard_map/ppermute | solution.py:19
  7.4 6.5 %fusion.80 = f32[64,24]{0,1:T(8,128)S(1)} fusion(f32[24,3,4,8,128]{4,3,2,1,0:T(8,128)S(1)} %copy-done.2, f32[64,3,4,8,128]{4,3,2,1,0:T(8,128)} %param.8), kind=kOutput, calls=%fused_computation.135 | convolution fusion | flops 226492416 | bytes 4331520 | tf_op jit(solution)/shard_map/dot_general | solution.py:111
  13.9 24.8 %psum.7 = f32[64,24]{0,1:T(8,128)S(1)} all-reduce(f32[64,24]{0,1:T(8,128)S(1)} %fusion.80), channel_id=1, replica_groups=mesh['prow'=8,'pcol'=4] {'prow'}, use_global_device_ids=true, to_apply=%region_0.1 | all-reduce | flops 1536 | bytes 12288 | tf_op jit(solution)/shard_map/psum | solution.py:114
  39.4 1.3 compare_select_fusion
  40.7 1.3 compare_select_fusion.1
  43.2 3.1 %fusion.130 = (f32[73,4,10,1]{3,2,1,0:T(8,128)}, f32[73,4,10,1]{3,2,1,0:T(8,128)}) fusion(f32[73,4,10,128]{3,2,1,0:T(8,128)S(1)} %pad_maximum_fusion.1), kind=kLoop, calls=%fused_computation.314 | loop fusion | bytes 46720 | tf_op jit(solution)/shard_map/slice | solution.py:17
  46.2 2.5 %copy.78 = f32[73,4,10,1]{0,1,3,2:T(4,128)S(1)} copy(f32[73,4,10,1]{3,2,1,0:T(8,128)} %get-tuple-element.62) | data formatting | bytes 23360 | tf_op jit(solution)/shard_map/slice | solution.py:18
  48.8 2.4 %collective-permute-start.3 = (f32[73,4,10,1]{0,1,3,2:T(4,128)S(1)}, f32[73,4,10,1]{0,1,3,2:T(4,128)S(1)}, u32[]{:S(2)}, u32[]{:S(2)}) collective-permute-start(f32[73,4,10,1]{0,1,3,2:T(4,128)S(1)} %copy.78), channel_id=1, source_target_pairs={{1,0},{2,1},{3,2},{5,4},{6,5},{7,6},{9,8},{10,9},{11,10},{13,12},{... | collective-permute-start | bytes 35048 | tf_op jit(solution)/shard_map/ppermute | solution.py:20
  51.1 2.5 %copy.77 = f32[73,4,10,1]{0,1,3,2:T(4,128)S(1)} copy(f32[73,4,10,1]{3,2,1,0:T(8,128)} %get-tuple-element.61) | data formatting | bytes 23360 | tf_op jit(solution)/shard_map/slice | solution.py:17
  53.7 3.7 %collective-permute-start.2 = (f32[73,4,10,1]{0,1,3,2:T(4,128)S(1)}, f32[73,4,10,1]{0,1,3,2:T(4,128)S(1)}, u32[]{:S(2)}, u32[]{:S(2)}) collective-permute-start(f32[73,4,10,1]{0,1,3,2:T(4,128)S(1)} %copy.77), channel_id=1, source_target_pairs={{0,1},{1,2},{2,3},{4,5},{5,6},{6,7},{8,9},{9,10},{10,11},{12,13},{... | collective-permute-start | bytes 35048 | tf_op jit(solution)/shard_map/ppermute | solution.py:19
  58.1 3.7 %copy.139 = f32[8,8,96,128]{3,1,2,0:T(8,128)S(1)} copy(f32[8,8,96,128]{3,2,1,0:T(8,128)} %bitcast.41) | data formatting | bytes 6291456
  61.8 2.2 %copy.121 = f32[8,8,96,128]{3,2,1,0:T(8,128)} copy(f32[8,8,96,128]{3,1,2,0:T(8,128)S(1)} %copy.139) | data formatting | bytes 6291456
  64.0 3.3 %copy.80 = f32[73,4,10,1]{3,2,1,0:T(8,128)} copy(f32[73,4,10,1]{0,1,3,2:T(4,128)S(1)} %collective-permute-done.3) | data formatting | bytes 23360 | tf_op jit(solution)/shard_map/ppermute | solution.py:20
  67.3 3.3 %copy.79 = f32[73,4,10,1]{3,2,1,0:T(8,128)} copy(f32[73,4,10,1]{0,1,3,2:T(4,128)S(1)} %collective-permute-done.2) | data formatting | bytes 23360 | tf_op jit(solution)/shard_map/ppermute | solution.py:19
  70.6 1.0 pad_maximum_fusion.4
  73.3 4.8 %pad_maximum_fusion = f32[73,4,10,130]{3,2,1,0:T(8,128)S(1)} fusion(f32[73,4,10,1]{3,2,1,0:T(8,128)S(1)} %copy-done.3, f32[73,4,1,128]{3,2,1,0:T(1,128)S(1)} %collective-permute-done.1, f32[1,4,8,128]{3,2,1,0:T(8,128)S(1)} %bitcast.46, f32[72,4,8,128]{3,2,1,0:T(8,128)S(1)} %bitcast.39, f32[73,4,1,128]{3,2,1,0:T(1,128)S(1)} %collective-permute-done, ...), kind=kLoop, calls=%fused_computation.18 | loop fusion | flops 1898000 | bytes 3036800 | tf_op jit(solution)/shard_map/concatenate | solution.py:21
  78.1 1.1 slice_multiply_fusion
  79.2 2.5 %copy_divide_fusion = f32[24,3,4,10,130]{4,0,3,2,1:T(8,128)S(1)} fusion(f32[24,3,4,10,130]{4,3,2,1,0:T(8,128)S(1)} %bitcast.40, f32[4,10,130]{2,1,0:T(8,128)S(1)} %copy.83), kind=kLoop, calls=%fused_computation.25 | loop fusion | flops 374400 | bytes 3016000 | tf_op jit(solution)/shard_map/div | solution.py:84
  81.7 2.6 %fusion.21 = (f32[24,3,4,8,128]{4,0,3,2,1:T(8,128)S(1)}, f32[24,3,4,8,128]{4,0,3,2,1:T(8,128)S(1)}, f32[24,3,4,8,128]{4,0,3,2,1:T(8,128)S(1)}, f32[24,3,4,8,128]...) fusion(f32[24,3,4,10,130]{4,0,3,2,1:T(8,128)S(1)} %copy_divide_fusion, ...), kind=kLoop, calls=%fused_computation.42 | loop fusion | flops 3538944 | bytes 13570080 | tf_op jit(solution)/shard_map/sub | solution.py:51
  84.3 1.1 multiply_add_fusion.4
  87.2 2.5 %fusion.17 = (f32[24,3,4,8,128]{4,0,3,2,1:T(8,128)S(1)}, f32[24,3,4,8,128]{4,0,3,2,1:T(8,128)S(1)}, f32[24,3,4,8,128]{4,0,3,2,1:T(8,128)}, f32[24,3,4,8,128]{4,0...) fusion(f32[24,3,4,10,130]{4,0,3,2,1:T(8,128)S(1)} %copy_divide_fusion, ...), kind=kLoop, calls=%fused_computation.38 | loop fusion | flops 3538944 | bytes 13570560 | tf_op jit(solution)/shard_map/sub | solution.py:51
  90.6 1.0 multiply_add_fusion.6
  91.6 1.1 multiply_add_fusion.10
  92.7 3.5 %fusion.8 = (f32[24,3,4,8,128]{4,0,3,2,1:T(8,128)S(1)}, f32[24,3,4,8,128]{4,0,3,2,1:T(8,128)S(1)}, f32[24,3,4,8,128]{4,0,3,2,1:T(8,128)}, f32[24,3,4,8,128]{4,0,...) fusion(f32[24,3,4,10,130]{4,0,3,2,1:T(8,128)S(1)} %copy_divide_, ...), kind=kLoop, calls=%fused_computation.29 | loop fusion | flops 4128768 | bytes 15929856 | tf_op jit(solution)/shard_map/sub | solution.py:51
  96.2 1.1 fusion.132
  97.3 2.9 %fusion.12 = (f32[24,3,4,8,128]{4,0,3,2,1:T(8,128)S(1)}, f32[24,3,4,8,128]{4,0,3,2,1:T(8,128)S(1)}, f32[24,3,4,8,128]{4,0,3,2,1:T(8,128)}, f32[24,3,4,8,128]{4,0...) fusion(f32[24,3,4,10,130]{4,0,3,2,1:T(8,128)S(1)} %copy_divide_fusion, ...), kind=kLoop, calls=%fused_computation.33 | loop fusion | flops 3538944 | bytes 13570560 | tf_op jit(solution)/shard_map/sub | solution.py:51
  100.2 2.3 %multiply_add_fusion.12 = (f32[24,1,4,8,128]{4,0,3,2,1:T(8,128)}, f32[24,1,4,8,128]{4,0,3,2,1:T(8,128)}, f32[24,1,4,8,128]{4,0,3,2,1:T(8,128)}) fusion(f32[24,3,4,8,128]{4,0,3,2,1:T(8,128)} %get-tuple-element.53), kind=kLoop, calls=%fused_computation.176 | loop fusion | flops 884736 | bytes 2359296 | tf_op jit(solution)/shard_map/add | solution.py:64
  103.3 1.0 multiply_add_fusion.15
  104.8 1.1 multiply_add_fusion.18
  107.8 1.1 slice_multiply_fusion.15
  108.9 1.0 slice_multiply_fusion.17
  110.6 1.1 slice_multiply_fusion.18
  112.3 1.0 slice_multiply_fusion.20
  114.0 1.1 slice_multiply_fusion.22
  115.7 1.1 slice_multiply_fusion.23
  117.4 1.1 slice_multiply_fusion.25
  119.1 1.1 slice_multiply_fusion.26
  121.1 1.1 multiply_add_fusion.35
  122.2 1.1 multiply_add_fusion.38
  125.1 1.1 multiply_add_fusion.45
  126.8 1.0 fusion.131
  127.8 1.1 multiply_add_fusion.48
  129.7 1.0 multiply_add_fusion.50
  131.3 1.1 multiply_add_fusion.54
  135.4 13.2 %fusion.4 = f32[24,3,4,8,128]{4,0,3,2,1:T(8,128)S(1)} fusion(f32[24,64,1,1,1]{1,0,4,3,2:T(8,128)} %convolution_bitcast_fusion, f32[3,4,8,128,64]{3,2,1,0,4:T(8,128)S(1)} %bitcast.42, f32[24,1,4,8,128]{4,0,3,2,1:T(8,128)S(1)} %copy-done.17, f32[24,1,4,8,128]{4,0,3,2,1:T(8,128)S(1)} %copy-done.18, f32[24,1,4,8,128]{4,0,3,2,1:T(8,128)S(1)} %copy-done.16, ...), kind=kOutput, calls=%fused_computation.27 | convolution fusion | flops 258932736 | bytes 37804032 | tf_op jit(solution)/shard_map/dot_general | solution.py:116
  148.6 1.2 copy.115
  (149 shorter events, 21.8 us)
Async XLA Ops:
  0.0 57.3 %copy-start = (f32[1,64,64]{2,1,0:T(8,128)S(1)}, f32[1,64,64]{2,1,0:T(8,128)}, u32[]{:S(2)}) copy-start(f32[1,64,64]{2,1,0:T(8,128)} %param.9) | copy-start | bytes 49156
  0.0 6.8 %copy-start.15 = (f32[4,8,128]{2,1,0:T(8,128)S(1)}, f32[4,8,128]{2,1,0:T(8,128)}, u32[]{:S(2)}) copy-start(f32[4,8,128]{2,1,0:T(8,128)} %param.6) | copy-start | bytes 49156
  0.0 7.4 %copy-start.2 = (f32[24,3,4,8,128]{4,3,2,1,0:T(8,128)S(1)}, f32[24,3,4,8,128]{4,3,2,1,0:T(8,128)}, u32[]{:S(2)}) copy-start(f32[24,3,4,8,128]{4,3,2,1,0:T(8,128)} %param.5) | copy-start | bytes 3538948
  2.1 40.6 %collective-permute-start.1 = (f32[73,4,1,128]{3,2,1,0:T(1,128)S(1)}, f32[73,4,1,128]{3,2,1,0:T(1,128)S(1)}, u32[]{:S(2)}, u32[]{:S(2)}) collective-permute-start(f32[73,4,1,128]{3,2,1,0:T(1,128)S(1)} %get-tuple-element.80), channel_id=1, source_target_pairs={{4,0},{8,4},{12,8},{16,12},{20,16},{24,20},{28,24},{5,1},{9,5},{13... | collective-permute-start | bytes 448520 | tf_op jit(solution)/shard_map/ppermute | solution.py:20
  4.8 37.8 %collective-permute-start = (f32[73,4,1,128]{3,2,1,0:T(1,128)S(1)}, f32[73,4,1,128]{3,2,1,0:T(1,128)S(1)}, u32[]{:S(2)}, u32[]{:S(2)}) collective-permute-start(f32[73,4,1,128]{3,2,1,0:T(1,128)S(1)} %get-tuple-element.79), channel_id=1, source_target_pairs={{0,4},{4,8},{8,12},{12,16},{16,20},{20,24},{24,28},{1,5},{5,9},{9,... | collective-permute-start | bytes 448520 | tf_op jit(solution)/shard_map/ppermute | solution.py:19
  7.4 31.4 %copy-start.47 = (s32[1,1,4]{2,1,0:T(1,128)S(1)}, s32[1,1,4]{2,1,0:T(1,128)}, u32[]{:S(2)}) copy-start(s32[1,1,4]{2,1,0:T(1,128)} %param.7) | copy-start | bytes 52
  40.7 2.5 %copy-start.42 = (f32[8]{0:T(128)}, f32[8]{0:T(128)S(1)}, u32[]{:S(2)}) copy-start(f32[8]{0:T(128)S(1)} %get-tuple-element.170) | copy-start | bytes 100
  40.7 2.5 %copy-start.46 = (f32[8]{0:T(128)}, f32[8]{0:T(128)S(1)}, u32[]{:S(2)}) copy-start(f32[8]{0:T(128)S(1)} %get-tuple-element.169) | copy-start | bytes 100
  42.0 1.2 copy-start.40
  42.0 1.2 copy-start.44
  48.8 15.2 %collective-permute-start.3 = (f32[73,4,10,1]{0,1,3,2:T(4,128)S(1)}, f32[73,4,10,1]{0,1,3,2:T(4,128)S(1)}, u32[]{:S(2)}, u32[]{:S(2)}) collective-permute-start(f32[73,4,10,1]{0,1,3,2:T(4,128)S(1)} %copy.78), channel_id=1, source_target_pairs={{1,0},{2,1},{3,2},{5,4},{6,5},{7,6},{9,8},{10,9},{11,10},{13,12},{... | collective-permute-start | bytes 35048 | tf_op jit(solution)/shard_map/ppermute | solution.py:20
  53.7 13.6 %collective-permute-start.2 = (f32[73,4,10,1]{0,1,3,2:T(4,128)S(1)}, f32[73,4,10,1]{0,1,3,2:T(4,128)S(1)}, u32[]{:S(2)}, u32[]{:S(2)}) collective-permute-start(f32[73,4,10,1]{0,1,3,2:T(4,128)S(1)} %copy.77), channel_id=1, source_target_pairs={{0,1},{1,2},{2,3},{4,5},{5,6},{6,7},{8,9},{9,10},{10,11},{12,13},{... | collective-permute-start | bytes 35048 | tf_op jit(solution)/shard_map/ppermute | solution.py:19
  70.6 2.7 %copy-start.3 = (f32[73,4,10,1]{3,2,1,0:T(8,128)S(1)}, f32[73,4,10,1]{3,2,1,0:T(8,128)}, u32[]{:S(2)}) copy-start(f32[73,4,10,1]{3,2,1,0:T(8,128)} %copy.80) | copy-start | bytes 35044
  70.6 2.7 %copy-start.4 = (f32[73,4,10,1]{3,2,1,0:T(8,128)S(1)}, f32[73,4,10,1]{3,2,1,0:T(8,128)}, u32[]{:S(2)}) copy-start(f32[73,4,10,1]{3,2,1,0:T(8,128)} %copy.79) | copy-start | bytes 35044
  91.6 1.1 copy-start.43
  103.3 1.6 %copy-start.13 = (f32[24,3,4,8,128]{4,0,3,2,1:T(8,128)S(1)}, f32[24,3,4,8,128]{4,0,3,2,1:T(8,128)}, u32[]{:S(2)}) copy-start(f32[24,3,4,8,128]{4,0,3,2,1:T(8,128)} %get-tuple-element.48) | copy-start | bytes 3538948
  108.9 1.7 %copy-start.6 = (f32[24,3,4,8,128]{4,0,3,2,1:T(8,128)S(1)}, f32[24,3,4,8,128]{4,0,3,2,1:T(8,128)}, u32[]{:S(2)}) copy-start(f32[24,3,4,8,128]{4,0,3,2,1:T(8,128)} %get-tuple-element.55) | copy-start | bytes 3538948
  110.6 1.7 %copy-start.5 = (f32[24,3,4,8,128]{4,0,3,2,1:T(8,128)S(1)}, f32[24,3,4,8,128]{4,0,3,2,1:T(8,128)}, u32[]{:S(2)}) copy-start(f32[24,3,4,8,128]{4,0,3,2,1:T(8,128)} %get-tuple-element.43) | copy-start | bytes 3538948
  112.3 1.7 %copy-start.8 = (f32[24,3,4,8,128]{4,0,3,2,1:T(8,128)S(1)}, f32[24,3,4,8,128]{4,0,3,2,1:T(8,128)}, u32[]{:S(2)}) copy-start(f32[24,3,4,8,128]{4,0,3,2,1:T(8,128)} %get-tuple-element.52) | copy-start | bytes 3538948
  114.0 1.7 %copy-start.7 = (f32[24,3,4,8,128]{4,0,3,2,1:T(8,128)S(1)}, f32[24,3,4,8,128]{4,0,3,2,1:T(8,128)}, u32[]{:S(2)}) copy-start(f32[24,3,4,8,128]{4,0,3,2,1:T(8,128)} %get-tuple-element.28) | copy-start | bytes 3538948
  115.7 1.7 %copy-start.12 = (f32[24,3,4,8,128]{4,0,3,2,1:T(8,128)S(1)}, f32[24,3,4,8,128]{4,0,3,2,1:T(8,128)}, u32[]{:S(2)}) copy-start(f32[24,3,4,8,128]{4,0,3,2,1:T(8,128)} %get-tuple-element.47) | copy-start | bytes 3538948
  117.4 1.7 %copy-start.11 = (f32[24,3,4,8,128]{4,0,3,2,1:T(8,128)S(1)}, f32[24,3,4,8,128]{4,0,3,2,1:T(8,128)}, u32[]{:S(2)}) copy-start(f32[24,3,4,8,128]{4,0,3,2,1:T(8,128)} %get-tuple-element.25) | copy-start | bytes 3538948
  125.1 1.7 %copy-start.10 = (f32[24,3,4,8,128]{4,0,3,2,1:T(8,128)S(1)}, f32[24,3,4,8,128]{4,0,3,2,1:T(8,128)}, u32[]{:S(2)}) copy-start(f32[24,3,4,8,128]{4,0,3,2,1:T(8,128)} %get-tuple-element.50) | copy-start | bytes 3538948
  128.9 6.0 %copy-start.28 = (f32[24,1,4,8,128]{4,0,3,2,1:T(8,128)S(1)}, f32[24,1,4,8,128]{4,0,3,2,1:T(8,128)}, u32[]{:S(2)}) copy-start(f32[24,1,4,8,128]{4,0,3,2,1:T(8,128)} %get-tuple-element.120) | copy-start | bytes 1179652
  129.7 1.6 %copy-start.9 = (f32[24,3,4,8,128]{4,0,3,2,1:T(8,128)S(1)}, f32[24,3,4,8,128]{4,0,3,2,1:T(8,128)}, u32[]{:S(2)}) copy-start(f32[24,3,4,8,128]{4,0,3,2,1:T(8,128)} %get-tuple-element.49) | copy-start | bytes 3538948
  129.7 5.2 %copy-start.26 = (f32[24,1,4,8,128]{4,0,3,2,1:T(8,128)S(1)}, f32[24,1,4,8,128]{4,0,3,2,1:T(8,128)}, u32[]{:S(2)}) copy-start(f32[24,1,4,8,128]{4,0,3,2,1:T(8,128)} %get-tuple-element.124) | copy-start | bytes 1179652
  129.7 5.2 %copy-start.27 = (f32[24,1,4,8,128]{4,0,3,2,1:T(8,128)S(1)}, f32[24,1,4,8,128]{4,0,3,2,1:T(8,128)}, u32[]{:S(2)}) copy-start(f32[24,1,4,8,128]{4,0,3,2,1:T(8,128)} %get-tuple-element.125) | copy-start | bytes 1179652
  131.3 3.7 %copy-start.20 = (f32[24,1,4,8,128]{4,0,3,2,1:T(8,128)S(1)}, f32[24,1,4,8,128]{4,0,3,2,1:T(8,128)}, u32[]{:S(2)}) copy-start(f32[24,1,4,8,128]{4,0,3,2,1:T(8,128)} %get-tuple-element.130) | copy-start | bytes 1179652
  131.3 3.7 %copy-start.21 = (f32[24,1,4,8,128]{4,0,3,2,1:T(8,128)S(1)}, f32[24,1,4,8,128]{4,0,3,2,1:T(8,128)}, u32[]{:S(2)}) copy-start(f32[24,1,4,8,128]{4,0,3,2,1:T(8,128)} %get-tuple-element.131) | copy-start | bytes 1179652
  131.3 3.7 %copy-start.22 = (f32[24,1,4,8,128]{4,0,3,2,1:T(8,128)S(1)}, f32[24,1,4,8,128]{4,0,3,2,1:T(8,128)}, u32[]{:S(2)}) copy-start(f32[24,1,4,8,128]{4,0,3,2,1:T(8,128)} %get-tuple-element.126) | copy-start | bytes 1179652
  131.3 3.7 %copy-start.23 = (f32[24,1,4,8,128]{4,0,3,2,1:T(8,128)S(1)}, f32[24,1,4,8,128]{4,0,3,2,1:T(8,128)}, u32[]{:S(2)}) copy-start(f32[24,1,4,8,128]{4,0,3,2,1:T(8,128)} %get-tuple-element.127) | copy-start | bytes 1179652
  131.3 3.7 %copy-start.24 = (f32[24,1,4,8,128]{4,0,3,2,1:T(8,128)S(1)}, f32[24,1,4,8,128]{4,0,3,2,1:T(8,128)}, u32[]{:S(2)}) copy-start(f32[24,1,4,8,128]{4,0,3,2,1:T(8,128)} %get-tuple-element.128) | copy-start | bytes 1179652
  131.3 3.7 %copy-start.25 = (f32[24,1,4,8,128]{4,0,3,2,1:T(8,128)S(1)}, f32[24,1,4,8,128]{4,0,3,2,1:T(8,128)}, u32[]{:S(2)}) copy-start(f32[24,1,4,8,128]{4,0,3,2,1:T(8,128)} %get-tuple-element.123) | copy-start | bytes 1179652
  132.4 2.3 %copy-start.33 = (f32[4,8,128]{2,0,1:T(4,128)S(1)}, f32[4,8,128]{2,0,1:T(4,128)}, u32[]{:S(2)}) copy-start(f32[4,8,128]{2,0,1:T(4,128)} %get-tuple-element.156) | copy-start | bytes 49156
  132.4 2.3 %copy-start.31 = (f32[4,8,128]{2,0,1:T(4,128)S(1)}, f32[4,8,128]{2,0,1:T(4,128)}, u32[]{:S(2)}) copy-start(f32[4,8,128]{2,0,1:T(4,128)} %get-tuple-element.157) | copy-start | bytes 49156
  132.4 2.4 %copy-start.29 = (f32[4,8,128]{2,0,1:T(4,128)S(1)}, f32[4,8,128]{2,0,1:T(4,128)}, u32[]{:S(2)}) copy-start(f32[4,8,128]{2,0,1:T(4,128)} %get-tuple-element.158) | copy-start | bytes 49156
  132.4 2.6 %copy-start.14 = (f32[8,8,96,128]{3,2,1,0:T(8,128)S(1)}, f32[8,8,96,128]{3,2,1,0:T(8,128)}, u32[]{:S(2)}) copy-start(f32[8,8,96,128]{3,2,1,0:T(8,128)} %copy.121) | copy-start | bytes 9437188
  133.2 1.3 copy-start.36
  133.2 1.3 copy-start.34
  133.3 1.3 copy-start.32
  133.3 1.3 copy-start.30
  133.3 1.4 copy-start.37
  133.3 1.4 copy-start.35
  133.3 1.8 %copy-start.16 = (f32[24,1,4,8,128]{4,0,3,2,1:T(8,128)S(1)}, f32[24,1,4,8,128]{4,0,3,2,1:T(8,128)}, u32[]{:S(2)}) copy-start(f32[24,1,4,8,128]{4,0,3,2,1:T(8,128)} %get-tuple-element.132) | copy-start | bytes 1179652
  133.3 1.9 %copy-start.17 = (f32[24,1,4,8,128]{4,0,3,2,1:T(8,128)S(1)}, f32[24,1,4,8,128]{4,0,3,2,1:T(8,128)}, u32[]{:S(2)}) copy-start(f32[24,1,4,8,128]{4,0,3,2,1:T(8,128)} %get-tuple-element.133) | copy-start | bytes 1179652
  133.3 2.0 %copy-start.18 = (f32[24,1,4,8,128]{4,0,3,2,1:T(8,128)S(1)}, f32[24,1,4,8,128]{4,0,3,2,1:T(8,128)}, u32[]{:S(2)}) copy-start(f32[24,1,4,8,128]{4,0,3,2,1:T(8,128)} %get-tuple-element.134) | copy-start | bytes 1179652
  133.3 2.1 %copy-start.19 = (f32[24,1,4,8,128]{4,0,3,2,1:T(8,128)S(1)}, f32[24,1,4,8,128]{4,0,3,2,1:T(8,128)}, u32[]{:S(2)}) copy-start(f32[24,1,4,8,128]{4,0,3,2,1:T(8,128)} %get-tuple-element.129) | copy-start | bytes 1179652
  135.4 14.5 %copy-start.1 = (f32[1,64,64]{2,1,0:T(8,128)S(1)}, f32[1,64,64]{2,1,0:T(8,128)}, u32[]{:S(2)}) copy-start(f32[1,64,64]{2,1,0:T(8,128)} %param.9) | copy-start | bytes 49156
  (4 other events, 4.2 us)
where the time goes:
time: 151 us; the launch traced here: 150 us
  other arithmetic  64.5 us (43%)
  local copies, waits for them, and re-layouts  28.7 us (19%)
  blocking collectives  24.8 us (16%)
  matrix products  20.5 us (14%)
  starting transfers between devices  10.7 us (7%)
    psum x1, blocking collectives, per_device(): restricted = lax.psum(partial_terms, 'prow')  24.8 us
    add x24, other arithmetic, bond_sum(): piece = piece + 0.4 * direction[component] / length * projected  24.7 us
    dot_general x1, matrix products, per_device(): lax.dot_general(solved, flat_vectors, (((0,), (0,)), ((), ())), precision...  13.2 us
    unnamed x98, local copies, waits for them, and re-layouts  12 us
    sub x4, other arithmetic, bond_sum(): difference = own_field - factor * near_field  11.5 us
    mul x8, other arithmetic, bond_sum(): piece = 0.6 * difference[..., component, :, :, :]  8.8 us
    dot_general x1, matrix products, per_device(): lax.dot_general(flat_vectors, flat_loads, (((1,), (1,)), ((), ())), preci...  6.54 us
    slice x2, local copies, waits for them, and re-layouts, extended(): last = lax.slice_in_dim(x, length - width, length, axis=dim)  5.6 us
  transfers between devices with their start and end apart: 4, of which 0 were waited for; matrix products, arithmetic and copies ran while one was open for 16% of the time, Pallas kernels for 0%

commit v1 on v0

v1 whole, which is shorter than its diff:
```python
import functools

import jax
import jax.numpy as jnp
import ml_dtypes
import numpy as np
from jax import lax
from jax.experimental import pallas as pl
from jax.experimental.pallas import tpu as pltpu
from jax.sharding import PartitionSpec as P

RELAX_WEIGHT = 0.7
MASS_SHIFT = 0.5
DIAGONAL_SLOPE = 0.6 + 0.4 / 3.0
SCALE = 660.0
MESH = pl.DeviceIdType.MESH
F32, BF16 = jnp.float32, jnp.bfloat16
PLANES, ROWS, LANES = 4, 8, 128
OFFSETS = [
    (p, x, y)
    for p in (-1, 0, 1)
    for x in (-1, 0, 1)
    for y in (-1, 0, 1)
    if (p, x, y) != (0, 0, 0)
]


def scaled_bond(d):
    length = sum(v * v for v in d)
    d = np.array(d, np.float64)
    return 27.0 / length * np.eye(3) + 18.0 / length**2 * np.outer(d, d)


def cell(c, p, x):
    return (c * PLANES + p) * ROWS + x


def constants():
    main = np.zeros((3, 96, 128))
    edge = np.zeros((3, 2, 96, 128))
    for d in OFFSETS:
        w = scaled_bond(d)
        dp, dx, dy = d
        for p in range(PLANES):
            q = p + dp
            if not 0 <= q < PLANES:
                continue
            for x in range(ROWS):
                z = x + dx
                for c in range(3):
                    for e in range(3):
                        row, v = cell(c, p, x), w[c, e]
                        if z < 0:
                            column, source, there = 96 + e * PLANES + q, 0, cell(e, q, ROWS - 1)
                        elif z >= ROWS:
                            column, source, there = 112 + e * PLANES + q, 2, cell(e, q, 0)
                        else:
                            column, source, there = cell(e, q, z), 1, cell(e, q, z)
                        main[dy + 1, row, column] += v
                        if dy:
                            edge[source, 0 if dy < 0 else 1, row, there] += v
    main = main.reshape(288, 128)
    edge = edge.reshape(3, 192, 128)
    place = np.zeros((3, 3, 32, 128))
    for dx in (-1, 0, 1):
        for p in range(PLANES):
            for x in range(ROWS):
                z = x + dx
                if z < 0:
                    place[0, dx + 1, p * ROWS + x, p * ROWS + ROWS - 1] = 1
                elif z >= ROWS:
                    place[2, dx + 1, p * ROWS + x, p * ROWS] = 1
                else:
                    place[1, dx + 1, p * ROWS + x, p * ROWS + z] = 1
    place = place.reshape(3, 96, 128)

    def twice(a):
        return np.concatenate([a, a], -1).astype(ml_dtypes.bfloat16)

    return twice(main), twice(edge), twice(place)


def halves(x):
    high = x.astype(BF16)
    return high, (x - high.astype(F32)).astype(BF16)


def dot(a, b):
    return jnp.dot(a, b, preferred_element_type=F32)


def dot_t(a, b):
    return lax.dot_general(a, b, (((1,), (1,)), ((), ())), preferred_element_type=F32)


def kernel(
    n, m, loads,
    sides_ref, r_hbm, v_hbm, mod_ref, inv_ref, main_ref, edge_ref, place_ref,
    out_ref,
    r_vm, v_vm, f_vm, xs, vs, row_out, row_in, col_out, col_in, part_out, part_in,
    in_sem, row_ssem, row_rsem, col_ssem, col_rsem, part_ssem, part_rsem,
):
    a, b = lax.axis_index("prow"), lax.axis_index("pcol")
    pairs = loads // 2
    vectors = v_hbm.shape[0]

    load_r = pltpu.make_async_copy(r_hbm, r_vm, in_sem.at[3])
    load_r.start()
    load_v = [
        pltpu.make_async_copy(v_hbm.at[:, c], v_vm.at[c], in_sem.at[c])
        for c in range(3)
    ]
    for copy in load_v:
        copy.start()

    barrier = pltpu.get_barrier_semaphore()
    for t in range(1, n):
        pl.semaphore_signal(barrier, inc=1, device_id=(lax.rem(a + t, n), b), device_id_type=MESH)
    beside = [(u, t) for u in (-1, 1) for t in (-1, 0, 1)]
    count = n - 1

    def there(t, u):
        ok = jnp.logical_and(a + t >= 0, a + t < n)
        return jnp.logical_and(ok, jnp.logical_and(b + u >= 0, b + u < m))

    for u, t in beside:
        count = count + there(t, u).astype(jnp.int32)

        @pl.when(there(t, u))
        def _(u=u, t=t):
            pl.semaphore_signal(barrier, inc=1, device_id=(a + t, b + u), device_id_type=MESH)

    mod = mod_ref[...]
    q = RELAX_WEIGHT / (MASS_SHIFT + DIAGONAL_SLOPE * mod)
    mod96 = jnp.concatenate([mod] * 3, 0)
    q96 = jnp.concatenate([q] * 3, 0)

    load_r.wait()
    mod_last = mod_ref[pl.ds(ROWS - 1, PLANES, stride=ROWS), :]
    mod_first = mod_ref[pl.ds(0, PLANES, stride=ROWS), :]

    def first_step(j, carry):
        for i in range(2):
            base = pl.multiple_of((2 * j + i) * 96, 96)
            lanes = slice(i * LANES, (i + 1) * LANES)
            f = r_vm[pl.ds(base, 96), :] * q96
            f_vm[pl.ds(base, 96), :] = f
            row_out[0, 2 * j + i, 0:12, :] = f_vm[pl.ds(base + ROWS - 1, 12, stride=ROWS), :]
            row_out[1, 2 * j + i, 0:12, :] = f_vm[pl.ds(base, 12, stride=ROWS), :]
            row_out[0, 2 * j + i, 12:16, :] = mod_last
            row_out[1, 2 * j + i, 12:16, :] = mod_first
            for g, x in enumerate((f, f * mod96)):
                high, low = halves(x)
                xs[j, g, 0:96, lanes] = high
                xs[j, g, 128:224, lanes] = low
        return carry

    lax.fori_loop(0, pairs, first_step, 0)

    pl.semaphore_wait(barrier, count)

    def row_copy(s):
        t = 1 if s == 0 else -1
        return pltpu.make_async_remote_copy(
            row_out.at[s], row_in.at[s], row_ssem.at[s], row_rsem.at[s],
            device_id=(a + t, b), device_id_type=MESH,
        )

    row_goes = [a + 1 < n, a >= 1]
    row_comes = [a >= 1, a + 1 < n]
    for s in range(2):
        pl.when(row_goes[s])(lambda s=s: row_copy(s).start())

    row48 = lax.broadcasted_iota(jnp.int32, (2 * loads, 2 * LANES), 0)
    lane48 = lax.broadcasted_iota(jnp.int32, (2 * loads, 2 * LANES), 1)
    side48 = (row48 >= loads).astype(jnp.int32)
    load48 = row48 - loads * side48
    odd = jnp.bitwise_and(load48, 1)
    pick_lane = odd * LANES + (1 - side48) * (LANES - 1)
    put_lane = odd * LANES + side48 * (LANES - 1)
    pick = (lane48 == pick_lane).astype(F32)
    put = (lane48 == put_lane).astype(F32)

    def column_step(j, carry):
        hot = jnp.where(load48 // 2 == j, pick, 0.0).astype(BF16)
        new = []
        for g in range(2):
            new.append(carry[g] + dot_t(hot, xs[j, g, 0:96, :]) + dot_t(hot, xs[j, g, 128:224, :]))
        return tuple(new)

    columns = lax.fori_loop(0, pairs, column_step, (jnp.zeros((2 * loads, 96), F32),) * 2)
    col_out[...] = jnp.zeros_like(col_out)
    row8 = lax.broadcasted_iota(jnp.int32, (16, LANES), 0)
    lane8 = lax.broadcasted_iota(jnp.int32, (16, LANES), 1)
    hot8 = (lane8 == jnp.where(row8 >= 8, 0, LANES - 1)).astype(F32).astype(BF16)
    mod_high, mod_low = halves(mod)
    mod_columns = dot_t(hot8, mod_high) + dot_t(hot8, mod_low)
    for s in range(2):
        for g in range(2):
            col_out[s, g * loads : (g + 1) * loads, 0:96] = columns[g][s * loads : (s + 1) * loads]
        col_out[s, 2 * loads :, 0:32] = mod_columns[8 * s : 8 * s + 8]

    def col_copy(u, t):
        s = 0 if u == 1 else 1
        return pltpu.make_async_remote_copy(
            col_out.at[s], col_in.at[s, 1 - t], col_ssem.at[s, 1 - t], col_rsem.at[s, 1 - t],
            device_id=(a + t, b + u), device_id_type=MESH,
        )

    for u, t in beside:
        pl.when(there(t, u))(lambda u=u, t=t: col_copy(u, t).start())

    total = jnp.zeros((2 * loads, 2 * vectors), F32)
    for c in range(3):
        load_v[c].wait()

        def restrict_step(j, total, c=c):
            left, right = [], []
            for i in range(2):
                v = v_vm.at[c].reshape(vectors * 32, LANES)[pl.ds(2 * j + i, vectors, stride=32), :]
                v_high, v_low = halves(v)
                right.append(jnp.concatenate([v_high, v_low], 0))
                r = r_vm[pl.ds(c * 32 + 2 * j + i, loads, stride=96), :]
                left.append(r)
            both = jnp.concatenate(right, 1)
            vs[c * 16 + j] = both
            r_high, r_low = halves(jnp.concatenate(left, 1))
            r_both = jnp.concatenate([r_high.astype(F32), r_low.astype(F32)], 0).astype(BF16)
            return total + dot_t(r_both, both)

        total = lax.fori_loop(0, 16, restrict_step, total)
    upper = total[0:loads]
    part = upper + pltpu.roll(upper, vectors, 1) + total[loads:]
    part_out[...] = part
    part_in[a] = part

    def part_copy(t):
        return pltpu.make_async_remote_copy(
            part_out, part_in.at[a], part_ssem.at[t - 1], part_rsem.at[t - 1],
            device_id=(lax.rem(a + t, n), b), device_id_type=MESH,
        )

    def part_arrival(t):
        source = lax.rem(a + n - t, n)
        return pltpu.make_async_remote_copy(
            part_out, part_in.at[source], part_ssem.at[t - 1], part_rsem.at[t - 1],
            device_id=(lax.rem(a + t, n), b), device_id_type=MESH,
        )

    for t in range(1, n):
        part_copy(t).start()

    side = [sides_ref[0, i].astype(F32) for i in range(4)]
    for s in range(2):
        pl.when(row_comes[s])(lambda s=s: row_copy(s).wait_recv())

        @pl.when(jnp.logical_not(row_comes[s]))
        def _(s=s):
            row_in[s] = jnp.zeros(row_in.shape[1:], F32)

    for u, t in beside:
        s, o = (0 if u == -1 else 1), 1 + t
        pl.when(there(t, u))(lambda u=u, t=t: col_copy(-u, -t).wait_recv())

        @pl.when(jnp.logical_not(there(t, u)))
        def _(s=s, o=o):
            col_in[s, o] = jnp.zeros(col_in.shape[2:], F32)

    edges = jnp.zeros((192, LANES), F32)
    places = jnp.zeros((96, 16), F32)
    gap = jnp.zeros((64 - 2 * loads, LANES), F32)
    for o in range(3):
        across = side[0] if o == 0 else side[1] if o == 2 else 1.0
        pieces = []
        for g in range(2):
            for s in range(2):
                pieces.append(col_in[s, o, g * loads : (g + 1) * loads, :] * (side[2 + s] * across))
            pieces.append(gap)
        high, low = halves(jnp.concatenate(pieces, 0))
        edges = edges + dot_t(edge_ref[o], jnp.concatenate([high, low], 1))
        high, low = halves(jnp.concatenate([col_in[0, o, 2 * loads :, :], col_in[1, o, 2 * loads :, :]], 0))
        places = places + dot_t(place_ref[o], jnp.concatenate([high, low], 1))
    lane = lax.broadcasted_iota(jnp.int32, (96, LANES), 1)
    from_left = jnp.logical_or(lane < loads, jnp.logical_and(lane >= 64, lane < 64 + loads))
    edges = jnp.where(from_left, edges[0:96], edges[96:192])
    own = jnp.where(lane < loads, mod96[:, 0:1], mod96[:, LANES - 1 :])
    edges = jnp.where(lane < 2 * loads, own * edges + pltpu.roll(edges, 64, 1), 0.0)
    edge_high, edge_low = halves(edges[:, 0 : 2 * loads])

    low_row, high_row = row_in[0, 0, 12:16, :], row_in[1, 0, 12:16, :]
    lane32 = lax.broadcasted_iota(jnp.int32, (32, LANES), 1)
    mod3 = mod.reshape(PLANES, ROWS, LANES)
    shifted = {}
    for dx in (-1, 0, 1):
        if dx == 0:
            base = mod
        elif dx < 0:
            base = jnp.concatenate(
                [z for p in range(PLANES) for z in (low_row[p : p + 1], mod3[p, 0 : ROWS - 1])], 0)
        else:
            base = jnp.concatenate(
                [z for p in range(PLANES) for z in (mod3[p, 1:ROWS], high_row[p : p + 1])], 0)
        here = places[(dx + 1) * 32 : (dx + 2) * 32]
        shifted[dx, 0] = base
        shifted[dx, -1] = jnp.where(lane32 == 0, here[:, 0:1], pltpu.roll(base, 1, 1))
        shifted[dx, 1] = jnp.where(lane32 == LANES - 1, here[:, 8:9], pltpu.roll(base, LANES - 1, 1))
    none = jnp.zeros((ROWS, LANES), F32)
    bonds = {}
    for d in OFFSETS:
        near = shifted[d[1], d[2]]
        if d[0] < 0:
            near = jnp.concatenate([none, near[0:24]], 0)
        elif d[0] > 0:
            near = jnp.concatenate([near[8:32], none], 0)
        w = scaled_bond(d)
        for c in range(3):
            for e in range(c, 3):
                if w[c, e]:
                    bonds[c, e] = bonds.get((c, e), 0.0) + float(w[c, e]) * near
    mix = {}
    for c in range(3):
        for e in range(c, 3):
            if c == e:
                total_bond = (0.5 / SCALE) * bonds[c, e] + (0.5 * DIAGONAL_SLOPE) * mod
                mix[c, e] = 2.0 - q * (MASS_SHIFT + total_bond)
            else:
                mix[c, e] = mix[e, c] = (-0.5 / SCALE) * q * bonds[c, e]
    rows = [jnp.concatenate([mix[c, e] for c in range(3)], 0) for e in range(3)]
    weight96 = (0.5 / SCALE) * q96
    before = pltpu.roll(mod96, LANES - 1, 1)
    after = pltpu.roll(mod96, 1, 1)
    none4 = jnp.zeros((4, LANES), F32)

    def halo_mod(s):
        row = row_in[s, 0, 12:16, :]
        return jnp.concatenate([row, row, row, none4], 0)

    halo_mods = [halo_mod(0), halo_mod(1)]

    def stencil_step(j, carry):
        for i in range(2):
            lanes = slice(i * LANES, (i + 1) * LANES)
            for s in range(2):
                f = row_in[s, 2 * j + i] * side[s]
                for g, x in enumerate((f, f * halo_mods[s])):
                    high, low = halves(x)
                    xs[j, g, 96 + 16 * s : 112 + 16 * s, lanes] = high
                    xs[j, g, 224 + 16 * s : 240 + 16 * s, lanes] = low
        hot = jnp.where(load48 // 2 == j, put, 0.0).astype(BF16)
        ends = dot(edge_high, hot) + dot(edge_low, hot)
        of = dot(main_ref[...], xs[j, 0])
        oh = dot(main_ref[...], xs[j, 1])
        for i in range(2):
            lanes = slice(i * LANES, (i + 1) * LANES)
            base = pl.multiple_of((2 * j + i) * 96, 96)
            low = pltpu.roll(of[0:96, lanes] * before + oh[0:96, lanes], 1, 1)
            mid = of[96:192, lanes] * mod96 + oh[96:192, lanes]
            high = pltpu.roll(of[192:288, lanes] * after + oh[192:288, lanes], LANES - 1, 1)
            near = mid + jnp.where(lane == 0, 0.0, low) + jnp.where(lane == LANES - 1, 0.0, high)
            near = near + ends[:, lanes]
            f = f_vm[pl.ds(base, 96), :]
            value = weight96 * near
            for e in range(3):
                value = value + rows[e] * jnp.concatenate([f[32 * e : 32 * e + 32]] * 3, 0)
            out_ref[pl.ds(base, 96), :] = value
        return carry

    lax.fori_loop(0, pairs, stencil_step, 0)

    for t in range(1, n):
        part_arrival(t).wait_recv()
    restricted = part_in[0]
    for t in range(1, n):
        restricted = restricted + part_in[t]
    r_high, r_low = halves(restricted[:, 0:vectors])
    i_high, i_low = halves(inv_ref[...])
    solved = dot_t(r_high, i_high) + dot_t(r_low, i_high) + dot_t(r_high, i_low)
    s_high, s_low = halves(solved)
    s_high, s_low = s_high.astype(F32), s_low.astype(F32)
    left = jnp.concatenate(
        [
            jnp.concatenate([s_high, s_high], 1),
            jnp.concatenate([s_low, jnp.zeros_like(s_low)], 1),
        ],
        0,
    ).astype(BF16)

    def lift_step(j, carry):
        both = dot(left, vs[j])
        sums = both[0:loads] + both[loads:]
        for i in range(2):
            place = pl.ds(2 * j + i, loads, stride=96)
            out_ref[place, :] = out_ref[place, :] + sums[:, i * LANES : (i + 1) * LANES]
        return carry

    lax.fori_loop(0, 48, lift_step, 0)

    for s in range(2):
        pl.when(row_goes[s])(lambda s=s: row_copy(s).wait_send())
    for u, t in beside:
        pl.when(there(t, u))(lambda u=u, t=t: col_copy(u, t).wait_send())
    for t in range(1, n):
        part_copy(t).wait_send()


def per_device(n, m, right_sides, modulus, margin_sides, coarse_vectors, coarse_inverse):
    loads, vectors = right_sides.shape[0], coarse_vectors.shape[0]
    main, edge, place = constants()
    vmem = pl.BlockSpec(memory_space=pltpu.VMEM)
    anywhere = pl.BlockSpec(memory_space=pl.ANY)
    message = (2 * loads + 8, LANES)
    dma = pltpu.SemaphoreType.DMA
    out = pl.pallas_call(
        functools.partial(kernel, n, m, loads),
        out_shape=jax.ShapeDtypeStruct((loads * 96, LANES), F32),
        in_specs=[pl.BlockSpec(memory_space=pltpu.SMEM), anywhere, anywhere] + [vmem] * 5,
        out_specs=vmem,
        scratch_shapes=[
            pltpu.VMEM((loads * 96, LANES), F32),
            pltpu.VMEM((3, vectors, 32, LANES), F32),
            pltpu.VMEM((loads * 96, LANES), F32),
            pltpu.VMEM((loads // 2, 2, 256, 2 * LANES), BF16),
            pltpu.VMEM((48, 2 * vectors, 2 * LANES), BF16),
            pltpu.VMEM((2, loads, 16, LANES), F32),
            pltpu.VMEM((2, loads, 16, LANES), F32),
            pltpu.VMEM((2,) + message, F32),
            pltpu.VMEM((2, 3) + message, F32),
            pltpu.VMEM((loads, 2 * vectors), F32),
            pltpu.VMEM((n, loads, 2 * vectors), F32),
            dma((4,)),
            dma((2,)),
            dma((2,)),
            dma((2, 3)),
            dma((2, 3)),
            dma((n - 1,)),
            dma((n - 1,)),
        ],
        compiler_params=pltpu.CompilerParams(
            collective_id=0, has_side_effects=True, vmem_limit_bytes=40 * 1024 * 1024
        ),
        cost_estimate=pl.CostEstimate(flops=10**9, bytes_accessed=6 * 10**6, transcendentals=0),
        name="schwarz",
    )(
        margin_sides.reshape(1, 4),
        right_sides.reshape(loads * 96, LANES),
        coarse_vectors.reshape(vectors, 3, 32, LANES),
        modulus.reshape(32, LANES),
        coarse_inverse.reshape(vectors, vectors),
        jnp.asarray(main),
        jnp.asarray(edge),
        jnp.asarray(place),
    )
    return out.reshape(right_sides.shape)


def solution(mesh):
    in_specs = (
        P(None, None, None, "prow", "pcol"),
        P(None, "prow", "pcol"),
        P("prow", "pcol", None),
        P(None, None, None, "prow", "pcol"),
        P("pcol", None, None),
    )
    out_specs = P(None, None, None, "prow", "pcol")
    return jax.shard_map(
        functools.partial(per_device, mesh.shape["prow"], mesh.shape["pcol"]),
        mesh=mesh, in_specs=in_specs, out_specs=out_specs, check_vma=False,
    )
```

time: 151 us -> 38.1 us (0.25)
  the two profiles are of different devices: /device:TPU:12 before, /device:TPU:0 now
where the time goes in v1:
time: 38.1 us; the launch traced here: 37.7 us
  Pallas kernels  28.6 us (75%)
  local copies, waits for them, and re-layouts  9.08 us (24%)
    pallas_call x1, Pallas kernels, per_device(): pl.pallas_call(functools.partial(kernel, n, m, loads), out_shape=jax.Shap...  28.6 us
    unnamed x17, local copies, waits for them, and re-layouts  9.08 us

profile of v1, /device:TPU:0, one launch (start us, length us, event | category | flops | bytes accessed | tf_op | source)
XLA Modules:
  0.0 37.7 jit_solution(15710024815687498139)
XLA Ops:
  0.0 0.0 copy-start
  0.0 1.9 %copy-done = f32[64,3,4,8,128]{4,3,2,1,0:T(8,128)S(1)} copy-done((f32[64,3,4,8,128]{4,3,2,1,0:T(8,128)S(1)}, f32[64,3,4,8,128]{4,3,2,1,0:T(8,128)}, u32[]{:S(2)}) %copy-start) | copy-done | bytes 3145752
  1.9 0.0 copy-start.1
  1.9 1.3 %copy-done.1 = f32[24,3,4,8,128]{4,3,2,1,0:T(8,128)S(1)} copy-done((f32[24,3,4,8,128]{4,3,2,1,0:T(8,128)S(1)}, f32[24,3,4,8,128]{4,3,2,1,0:T(8,128)}, u32[]{:S(2)}) %copy-start.1) | copy-done | bytes 1179672
  3.2 0.0 copy-start.2
  3.2 1.0 %copy-done.2 = bf16[3,192,256]{2,1,0:T(8,128)(2,1)S(1)} copy-done((bf16[3,192,256]{2,1,0:T(8,128)(2,1)S(1)}, bf16[3,192,256]{2,1,0:T(8,128)(2,1)}, u32[]{:S(2)}) %copy-start.2) | copy-done | bytes 294936
  4.1 0.0 copy-start.3
  4.1 0.9 %copy-done.3 = bf16[3,96,256]{2,1,0:T(8,128)(2,1)S(1)} copy-done((bf16[3,96,256]{2,1,0:T(8,128)(2,1)S(1)}, bf16[3,96,256]{2,1,0:T(8,128)(2,1)}, u32[]{:S(2)}) %copy-start.3) | copy-done | bytes 147480
  5.0 0.0 copy-start.4
  5.0 0.9 %copy-done.4 = bf16[288,256]{1,0:T(8,128)(2,1)S(1)} copy-done((bf16[288,256]{1,0:T(8,128)(2,1)S(1)}, bf16[288,256]{1,0:T(8,128)(2,1)}, u32[]{:S(2)}) %copy-start.4) | copy-done | bytes 147480
  5.9 0.0 copy-start.5
  5.9 0.8 %copy-done.5 = f32[1,64,64]{2,1,0:T(8,128)S(1)} copy-done((f32[1,64,64]{2,1,0:T(8,128)S(1)}, f32[1,64,64]{2,1,0:T(8,128)}, u32[]{:S(2)}) %copy-start.5) | copy-done | bytes 16408
  6.7 0.0 copy-start.6
  6.7 0.7 %copy-done.6 = f32[4,8,128]{2,1,0:T(8,128)S(1)} copy-done((f32[4,8,128]{2,1,0:T(8,128)S(1)}, f32[4,8,128]{2,1,0:T(8,128)}, u32[]{:S(2)}) %copy-start.6) | copy-done | bytes 16408
  7.4 0.0 copy-start.7
  7.4 0.7 %copy-done.7 = s32[1,1,4]{2,1,0:T(1,128)S(1)} copy-done((s32[1,1,4]{2,1,0:T(1,128)S(1)}, s32[1,1,4]{2,1,0:T(1,128)}, u32[]{:S(2)}) %copy-start.7) | copy-done | bytes 40
  8.1 28.6 %schwarz.1 = f32[2304,128]{1,0:T(8,128)S(1)} custom-call(s32[1,4]{1,0:T(1,128)S(1)} %bitcast.11, f32[2304,128]{1,0:T(8,128)S(1)} %bitcast.8, f32[64,3,32,128]{3,2,1,0:T(8,128)S(1)} %bitcast.7, f32[32,128]{1,0:T(8,128)S(1)} %bitcast.10, f32[64,64]{1,0:T(8,128)S(1)} %bitcast.9, bf16[288,256]{1,0:T(8,128)(2,1)S(1)} %copy-done.4, ...), custom_call_target="tpu_custom_call" | custom-call | flops 1000000000 | bytes 6000000 | tf_op jit(solution)/shard_map/schwarz/pallas_call | solution.py:413
  36.7 1.0 %copy.10 = f32[24,3,4,8,128]{4,3,2,1,0:T(8,128)} copy(f32[24,3,4,8,128]{4,3,2,1,0:T(8,128)S(1)} %bitcast.6) | data formatting | bytes 2359296
Async XLA Ops:
  0.0 1.9 %copy-start = (f32[64,3,4,8,128]{4,3,2,1,0:T(8,128)S(1)}, f32[64,3,4,8,128]{4,3,2,1,0:T(8,128)}, u32[]{:S(2)}) copy-start(f32[64,3,4,8,128]{4,3,2,1,0:T(8,128)} %param.11) | copy-start | bytes 9437188
  1.9 1.3 %copy-start.1 = (f32[24,3,4,8,128]{4,3,2,1,0:T(8,128)S(1)}, f32[24,3,4,8,128]{4,3,2,1,0:T(8,128)}, u32[]{:S(2)}) copy-start(f32[24,3,4,8,128]{4,3,2,1,0:T(8,128)} %param.8) | copy-start | bytes 3538948
  3.2 1.0 %copy-start.2 = (bf16[3,192,256]{2,1,0:T(8,128)(2,1)S(1)}, bf16[3,192,256]{2,1,0:T(8,128)(2,1)}, u32[]{:S(2)}) copy-start(bf16[3,192,256]{2,1,0:T(8,128)(2,1)} %constant.7.clone.edge_ref) | copy-start | bytes 884740
  4.1 0.9 %copy-start.3 = (bf16[3,96,256]{2,1,0:T(8,128)(2,1)S(1)}, bf16[3,96,256]{2,1,0:T(8,128)(2,1)}, u32[]{:S(2)}) copy-start(bf16[3,96,256]{2,1,0:T(8,128)(2,1)} %constant.8.clone.place_ref) | copy-start | bytes 442372
  5.0 0.9 %copy-start.4 = (bf16[288,256]{1,0:T(8,128)(2,1)S(1)}, bf16[288,256]{1,0:T(8,128)(2,1)}, u32[]{:S(2)}) copy-start(bf16[288,256]{1,0:T(8,128)(2,1)} %constant.6.clone.main_ref) | copy-start | bytes 442372
  5.9 0.8 %copy-start.5 = (f32[1,64,64]{2,1,0:T(8,128)S(1)}, f32[1,64,64]{2,1,0:T(8,128)}, u32[]{:S(2)}) copy-start(f32[1,64,64]{2,1,0:T(8,128)} %param.12) | copy-start | bytes 49156
  6.7 0.7 %copy-start.6 = (f32[4,8,128]{2,1,0:T(8,128)S(1)}, f32[4,8,128]{2,1,0:T(8,128)}, u32[]{:S(2)}) copy-start(f32[4,8,128]{2,1,0:T(8,128)} %param.9) | copy-start | bytes 49156
  7.4 0.7 %copy-start.7 = (s32[1,1,4]{2,1,0:T(1,128)S(1)}, s32[1,1,4]{2,1,0:T(1,128)}, u32[]{:S(2)}) copy-start(s32[1,1,4]{2,1,0:T(1,128)} %param.10) | copy-start | bytes 52

commit v2 on v1

--- a/solution.py
+++ b/solution.py
@@ -95,22 +95,31 @@
 
 def kernel(
     n, m, loads,
-    sides_ref, r_hbm, v_hbm, mod_ref, inv_ref, main_ref, edge_ref, place_ref,
+    sides_hbm, r_hbm, v_hbm, mod_hbm, inv_hbm, main_hbm, edge_hbm, place_hbm,
     out_ref,
-    r_vm, v_vm, f_vm, xs, vs, row_out, row_in, col_out, col_in, part_out, part_in,
+    sides_ref, mod_ref, inv_ref, main_ref, edge_ref, place_ref, r_vm, v_vm, f_vm, xs, vs, row_out, row_in, col_out, col_in, part_out, part_in,
     in_sem, row_ssem, row_rsem, col_ssem, col_rsem, part_ssem, part_rsem,
 ):
     a, b = lax.axis_index("prow"), lax.axis_index("pcol")
     pairs = loads // 2
     vectors = v_hbm.shape[0]
 
+    load_mod = pltpu.make_async_copy(mod_hbm, mod_ref, in_sem.at[4])
+    load_mod.start()
     load_r = pltpu.make_async_copy(r_hbm, r_vm, in_sem.at[3])
     load_r.start()
     load_v = [
         pltpu.make_async_copy(v_hbm.at[:, c], v_vm.at[c], in_sem.at[c])
         for c in range(3)
     ]
-    for copy in load_v:
+    load_rest = [
+        pltpu.make_async_copy(source, target, in_sem.at[5 + i])
+        for i, (source, target) in enumerate((
+            (sides_hbm, sides_ref), (inv_hbm, inv_ref), (main_hbm, main_ref),
+            (edge_hbm, edge_ref), (place_hbm, place_ref),
+        ))
+    ]
+    for copy in load_v + load_rest:
         copy.start()
 
     barrier = pltpu.get_barrier_semaphore()
@@ -130,6 +139,7 @@
         def _(u=u, t=t):
             pl.semaphore_signal(barrier, inc=1, device_id=(a + t, b + u), device_id_type=MESH)
 
+    load_mod.wait()
     mod = mod_ref[...]
     q = RELAX_WEIGHT / (MASS_SHIFT + DIAGONAL_SLOPE * mod)
     mod96 = jnp.concatenate([mod] * 3, 0)
@@ -155,7 +165,7 @@
                 xs[j, g, 128:224, lanes] = low
         return carry
 
-    lax.fori_loop(0, pairs, first_step, 0)
+    lax.fori_loop(0, pairs, first_step, 0, unroll=2)
 
     pl.semaphore_wait(barrier, count)
 
@@ -188,7 +198,7 @@
             new.append(carry[g] + dot_t(hot, xs[j, g, 0:96, :]) + dot_t(hot, xs[j, g, 128:224, :]))
         return tuple(new)
 
-    columns = lax.fori_loop(0, pairs, column_step, (jnp.zeros((2 * loads, 96), F32),) * 2)
+    columns = lax.fori_loop(0, pairs, column_step, (jnp.zeros((2 * loads, 96), F32),) * 2, unroll=4)
     col_out[...] = jnp.zeros_like(col_out)
     row8 = lax.broadcasted_iota(jnp.int32, (16, LANES), 0)
     lane8 = lax.broadcasted_iota(jnp.int32, (16, LANES), 1)
@@ -215,20 +225,24 @@
         load_v[c].wait()
 
         def restrict_step(j, total, c=c):
-            left, right = [], []
-            for i in range(2):
-                v = v_vm.at[c].reshape(vectors * 32, LANES)[pl.ds(2 * j + i, vectors, stride=32), :]
-                v_high, v_low = halves(v)
-                right.append(jnp.concatenate([v_high, v_low], 0))
-                r = r_vm[pl.ds(c * 32 + 2 * j + i, loads, stride=96), :]
-                left.append(r)
-            both = jnp.concatenate(right, 1)
-            vs[c * 16 + j] = both
-            r_high, r_low = halves(jnp.concatenate(left, 1))
-            r_both = jnp.concatenate([r_high.astype(F32), r_low.astype(F32)], 0).astype(BF16)
-            return total + dot_t(r_both, both)
-
-        total = lax.fori_loop(0, 16, restrict_step, total)
+            blocks = []
+            for h in range(4):
+                left, right = [], []
+                for i in range(2):
+                    at = 8 * j + 2 * h + i
+                    v = v_vm.at[c].reshape(vectors * 32, LANES)[pl.ds(at, vectors, stride=32), :]
+                    v_high, v_low = halves(v)
+                    right.append(jnp.concatenate([v_high, v_low], 0))
+                    left.append(r_vm[pl.ds(c * 32 + at, loads, stride=96), :])
+                r_high, r_low = halves(jnp.concatenate(left, 1))
+                r_both = jnp.concatenate([r_high.astype(F32), r_low.astype(F32)], 0).astype(BF16)
+                blocks.append((r_both, jnp.concatenate(right, 1)))
+            for h, (r_both, both) in enumerate(blocks):
+                vs[c * 16 + 4 * j + h] = both
+                total = total + dot_t(r_both, both)
+            return total
+
+        total = lax.fori_loop(0, 4, restrict_step, total)
     upper = total[0:loads]
     part = upper + pltpu.roll(upper, vectors, 1) + total[loads:]
     part_out[...] = part
@@ -250,7 +264,9 @@
     for t in range(1, n):
         part_copy(t).start()
 
-    side = [sides_ref[0, i].astype(F32) for i in range(4)]
+    for copy in load_rest:
+        copy.wait()
+    side = [sides_ref[0:1, i : i + 1].astype(F32) for i in range(4)]
     for s in range(2):
         pl.when(row_comes[s])(lambda s=s: row_copy(s).wait_recv())
 
@@ -270,7 +286,7 @@
     places = jnp.zeros((96, 16), F32)
     gap = jnp.zeros((64 - 2 * loads, LANES), F32)
     for o in range(3):
-        across = side[0] if o == 0 else side[1] if o == 2 else 1.0
+        across = side[0] if o == 0 else side[1] if o == 2 else jnp.ones_like(side[0])
         pieces = []
         for g in range(2):
             for s in range(2):
@@ -386,14 +402,18 @@
     ).astype(BF16)
 
     def lift_step(j, carry):
-        both = dot(left, vs[j])
-        sums = both[0:loads] + both[loads:]
-        for i in range(2):
-            place = pl.ds(2 * j + i, loads, stride=96)
-            out_ref[place, :] = out_ref[place, :] + sums[:, i * LANES : (i + 1) * LANES]
+        values = []
+        for h in range(8):
+            both = dot(left, vs[8 * j + h])
+            sums = both[0:loads] + both[loads:]
+            for i in range(2):
+                place = pl.ds(16 * j + 2 * h + i, loads, stride=96)
+                values.append((place, out_ref[place, :] + sums[:, i * LANES : (i + 1) * LANES]))
+        for place, value in values:
+            out_ref[place, :] = value
         return carry
 
-    lax.fori_loop(0, 48, lift_step, 0)
+    lax.fori_loop(0, 6, lift_step, 0)
 
     for s in range(2):
         pl.when(row_goes[s])(lambda s=s: row_copy(s).wait_send())
@@ -407,15 +427,20 @@
     loads, vectors = right_sides.shape[0], coarse_vectors.shape[0]
     main, edge, place = constants()
     vmem = pl.BlockSpec(memory_space=pltpu.VMEM)
-    anywhere = pl.BlockSpec(memory_space=pl.ANY)
     message = (2 * loads + 8, LANES)
     dma = pltpu.SemaphoreType.DMA
     out = pl.pallas_call(
         functools.partial(kernel, n, m, loads),
         out_shape=jax.ShapeDtypeStruct((loads * 96, LANES), F32),
-        in_specs=[pl.BlockSpec(memory_space=pltpu.SMEM), anywhere, anywhere] + [vmem] * 5,
+        in_specs=[pl.BlockSpec(memory_space=pltpu.HBM)] * 8,
         out_specs=vmem,
         scratch_shapes=[
+            pltpu.VMEM((1, 4), jnp.int32),
+            pltpu.VMEM((32, LANES), F32),
+            pltpu.VMEM((vectors, vectors), F32),
+            pltpu.VMEM(main.shape, BF16),
+            pltpu.VMEM(edge.shape, BF16),
+            pltpu.VMEM(place.shape, BF16),
             pltpu.VMEM((loads * 96, LANES), F32),
             pltpu.VMEM((3, vectors, 32, LANES), F32),
             pltpu.VMEM((loads * 96, LANES), F32),
@@ -427,7 +452,7 @@
             pltpu.VMEM((2, 3) + message, F32),
             pltpu.VMEM((loads, 2 * vectors), F32),
             pltpu.VMEM((n, loads, 2 * vectors), F32),
-            dma((4,)),
+            dma((10,)),
             dma((2,)),
             dma((2,)),
             dma((2, 3)),
@@ -436,7 +461,7 @@
             dma((n - 1,)),
         ],
         compiler_params=pltpu.CompilerParams(
-            collective_id=0, has_side_effects=True, vmem_limit_bytes=40 * 1024 * 1024
+            collective_id=0, has_side_effects=True, vmem_limit_bytes=58 * 1024 * 1024
         ),
         cost_estimate=pl.CostEstimate(flops=10**9, bytes_accessed=6 * 10**6, transcendentals=0),
         name="schwarz",

time: 38.1 us -> 22 us (0.58)
  the two profiles are of different devices: /device:TPU:0 before, /device:TPU:12 now
where the time goes in v2:
time: 22 us; the launch traced here: 21.7 us
  Pallas kernels  19.3 us (88%)
  local copies, waits for them, and re-layouts  2.37 us (11%)
    pallas_call x1, Pallas kernels, per_device(): pl.pallas_call(functools.partial(kernel, n, m, loads), out_shape=jax.Shap...  19.3 us
    unnamed x1, local copies, waits for them, and re-layouts  2.37 us

profile of v2, /device:TPU:12, one launch (start us, length us, event | category | flops | bytes accessed | tf_op | source)
XLA Modules:
  0.0 21.7 jit_solution(1578610483870140324)
XLA Ops:
  0.0 19.3 %schwarz.1 = f32[2304,128]{1,0:T(8,128)} custom-call(s32[1,4]{1,0:T(1,128)} %bitcast.11, f32[2304,128]{1,0:T(8,128)} %bitcast.8, f32[64,3,32,128]{3,2,1,0:T(8,128)} %bitcast.7, f32[32,128]{1,0:T(8,128)} %bitcast.10, f32[64,64]{1,0:T(8,128)} %bitcast.9, bf16[288,256]{1,0:T(8,128)(2,1)} %constant.6.clone.main_hbm, ...), custom_call_target="tpu_custom_call" | custom-call | flops 1000000000 | bytes 6000000 | tf_op jit(solution)/shard_map/schwarz/pallas_call | solution.py:432
  19.3 2.4 %copy.10 = f32[24,3,4,8,128]{4,3,2,1,0:T(8,128)} copy(f32[24,3,4,8,128]{4,3,2,1,0:T(8,128)} %bitcast.6) | data formatting | bytes 2359296
